TPU v7x, 1024 devices: a whole 8x8x8 slice. The times are simulated.
1024 devices in a mesh: dp: 32 (over y_lo, x), fsdp: 32 (over y_hi, z, core).
Axes of the slice: x: 8, y: 8 (y_hi: 2, y_lo: 4; y = y_hi * 4 + y_lo), z: 8, core: 2. Of those that a mesh axis runs over, the one named last changes fastest.
Arguments:
- q_raw: bfloat16 [32, 32, 128, 1664], P('dp', 'fsdp'), may hold values from -6 to 6
- k_raw: bfloat16 [32, 32, 128, 1664], P('dp', 'fsdp'), may hold values from -6 to 6
- v_raw: bfloat16 [32, 32, 128, 1664], P('dp', 'fsdp'), may hold values from -6 to 6
- gain_q: float32 [1664], P('fsdp'), may hold values from 0.1 to 1.9
- gain_k: float32 [1664], P('fsdp'), may hold values from 0.1 to 1.9
- dest: int32 [32, 32, 128], P('dp', 'fsdp'), may hold values from 0 to 31, as said below
- slot: int32 [32, 32, 128], P('dp', 'fsdp'), may hold values from 0 to 4, as said below
- recv_image: int32 [32, 32, 160], P('dp', 'fsdp'), may hold values from -1 to 1, as said below
- d_attended: bfloat16 [32, 32, 160, 1664], P('dp', 'fsdp'), may hold values from -6 to 6
Outputs:
- attended: bfloat16 [32, 32, 160, 1664], P('dp', 'fsdp')
- grad_q: bfloat16 [32, 32, 128, 1664], P('dp', 'fsdp')
- grad_k: bfloat16 [32, 32, 128, 1664], P('dp', 'fsdp')
- grad_v: bfloat16 [32, 32, 128, 1664], P('dp', 'fsdp')
- grad_gain_q: float32 [1664], P('fsdp')
- grad_gain_k: float32 [1664], P('fsdp')
Inputs may be any that keep to these rules, and one draw needn't show every extreme that they name: `dest`: from one device at most 5 tokens go to one destination, and in every device all 5 slots of some destination are used. No two tokens of one device share both dest and slot. `recv_image`: A received slot i * 5 + c holds -1 exactly when no token of device i is sent to that slot, else the image number of its token; all tokens that one device sends to one destination belong to one image.
All inputs are finite; a program needn't handle non-finite values.
Results may differ from a plain program's by a relative error of at most 0.0085.
Values may be sent and summed in bfloat16 or wider, within the bound.
A program may use at most 64 MiB of HBM per device.

v0:
```python
import jax
import jax.numpy as jnp
from jax import lax
from jax.sharding import PartitionSpec as P

HDIM = 128


def row_inverse(raw_rows):
    as_float = raw_rows.astype(jnp.float32)
    return lax.rsqrt(jnp.mean(as_float * as_float, axis=-1, keepdims=True) + 1e-06)


def normalized(raw_rows, inverse, gain_full):
    return (raw_rows.astype(jnp.float32) * inverse * gain_full).astype(jnp.bfloat16)


def restore_rows(grad_norm, raw_rows, inverse, gain_full):
    unit_rows = raw_rows.astype(jnp.float32) * inverse
    partial_sum = jnp.sum(grad_norm * unit_rows, axis=0)
    grad_unit = grad_norm * gain_full
    grad_raw = inverse * (
        grad_unit - unit_rows * jnp.mean(grad_unit * unit_rows, axis=-1, keepdims=True)
    )
    return (grad_raw, partial_sum)


def heads_first(rows, head_count):
    return rows.reshape(rows.shape[0], head_count, HDIM).transpose(1, 0, 2)


def rows_back(heads):
    head_count, slot_count, head_size = heads.shape
    return heads.transpose(1, 0, 2).reshape(slot_count, head_count * head_size)


def attend_block(query_norm, key_norm, value_rows, segments, grad_out):
    slot_count, feature_width = query_norm.shape
    head_count = feature_width // HDIM
    scaling = 1.0 / HDIM**0.5
    query_heads = heads_first(query_norm, head_count)
    key_heads = heads_first(key_norm, head_count)
    value_heads = heads_first(value_rows, head_count)
    grad_heads = heads_first(grad_out, head_count)
    allowed = ((segments[:, None] == segments[None, :]) & (segments[None, :] >= 0))[None]
    scores = jnp.einsum("hqd,hkd->hqk", query_heads, key_heads, preferred_element_type=jnp.float32)
    scores = jnp.where(allowed, scores * scaling, -1e30)
    highest = jnp.max(scores, axis=-1, keepdims=True)
    weights = jnp.where(allowed, jnp.exp(scores - highest), 0.0)
    denominator = jnp.sum(weights, axis=-1, keepdims=True)
    probs = weights / jnp.where(denominator > 0, denominator, 1.0)
    probs_low = probs.astype(jnp.bfloat16)
    attended = jnp.einsum(
        "hqk,hkd->hqd", probs_low, value_heads, preferred_element_type=jnp.float32
    )
    attended = rows_back(attended.astype(jnp.bfloat16))
    grad_probs = jnp.einsum(
        "hqd,hkd->hqk", grad_heads, value_heads, preferred_element_type=jnp.float32
    )
    grad_values = jnp.einsum(
        "hqk,hqd->hkd", probs_low, grad_heads, preferred_element_type=jnp.float32
    )
    grad_values = rows_back(grad_values.astype(jnp.bfloat16))
    inner = jnp.sum(grad_probs * probs, axis=-1, keepdims=True)
    grad_scores = (probs * (grad_probs - inner) * scaling).astype(jnp.bfloat16)
    grad_query = jnp.einsum(
        "hqk,hkd->hqd", grad_scores, key_heads, preferred_element_type=jnp.float32
    )
    grad_key = jnp.einsum(
        "hqk,hqd->hkd", grad_scores, query_heads, preferred_element_type=jnp.float32
    )
    return (attended, rows_back(grad_query), rows_back(grad_key), grad_values)


def shards(q_raw, k_raw, v_raw, gain_q, gain_k, dest, slot, recv_image, d_attended):
    tokens = q_raw.shape[2]
    feature_width = q_raw.shape[3]
    segments = recv_image.reshape(-1)
    slot_count = segments.shape[0]
    group_size = lax.axis_size("dp")
    capacity = slot_count // group_size
    route_index = dest.reshape(-1) * capacity + slot.reshape(-1)
    route_table = (jnp.arange(slot_count, dtype=jnp.int32)[:, None] == route_index[None, :]).astype(
        jnp.bfloat16
    )
    query_home = q_raw.reshape(tokens, feature_width)
    key_home = k_raw.reshape(tokens, feature_width)
    value_home = v_raw.reshape(tokens, feature_width)
    grad_out = d_attended.reshape(slot_count, feature_width)
    full_q, full_k = (
        lax.all_gather(gain_q, "fsdp", axis=0, tiled=True),
        lax.all_gather(gain_k, "fsdp", axis=0, tiled=True),
    )

    def placed(values_in):
        return jnp.dot(route_table, values_in, preferred_element_type=jnp.float32).astype(
            jnp.bfloat16
        )

    arrived = (
        lax.all_to_all(placed(query_home), "dp", split_axis=0, concat_axis=0, tiled=True),
        lax.all_to_all(placed(key_home), "dp", split_axis=0, concat_axis=0, tiled=True),
        lax.all_to_all(placed(value_home), "dp", split_axis=0, concat_axis=0, tiled=True),
    )
    inverse_q = row_inverse(arrived[0])
    inverse_k = row_inverse(arrived[1])
    query_norm = normalized(arrived[0], inverse_q, full_q)
    key_norm = normalized(arrived[1], inverse_k, full_k)
    attended, grad_qn, grad_kn, grad_values = attend_block(
        query_norm, key_norm, arrived[2], segments, grad_out
    )
    grad_qr, part_q = restore_rows(grad_qn, arrived[0], inverse_q, full_q)
    grad_kr, part_k = restore_rows(grad_kn, arrived[1], inverse_k, full_k)
    returned = (
        lax.all_to_all(grad_qr.astype(jnp.bfloat16), "dp", split_axis=0, concat_axis=0, tiled=True),
        lax.all_to_all(grad_kr.astype(jnp.bfloat16), "dp", split_axis=0, concat_axis=0, tiled=True),
        lax.all_to_all(grad_values, "dp", split_axis=0, concat_axis=0, tiled=True),
    )
    grad_query = jnp.take(returned[0], route_index, axis=0)
    grad_key = jnp.take(returned[1], route_index, axis=0)
    grad_value = jnp.take(returned[2], route_index, axis=0)
    shares = (
        lax.psum_scatter(part_q, "fsdp", scatter_dimension=0, tiled=True),
        lax.psum_scatter(part_k, "fsdp", scatter_dimension=0, tiled=True),
    )
    totals = lax.psum((shares[0], shares[1]), "dp")
    return (
        attended.reshape(1, 1, slot_count, feature_width),
        grad_query.reshape(1, 1, tokens, feature_width),
        grad_key.reshape(1, 1, tokens, feature_width),
        grad_value.reshape(1, 1, tokens, feature_width),
        totals[0],
        totals[1],
    )


def solution(mesh):
    return jax.shard_map(
        shards,
        mesh=mesh,
        in_specs=(
            P("dp", "fsdp", None, None),
            P("dp", "fsdp", None, None),
            P("dp", "fsdp", None, None),
            P("fsdp"),
            P("fsdp"),
            P("dp", "fsdp", None),
            P("dp", "fsdp", None),
            P("dp", "fsdp", None),
            P("dp", "fsdp", None, None),
        ),
        out_specs=(
            P("dp", "fsdp", None, None),
            P("dp", "fsdp", None, None),
            P("dp", "fsdp", None, None),
            P("dp", "fsdp", None, None),
            P("fsdp"),
            P("fsdp"),
        ),
        check_vma=False,
    )
```

profile of v0, /device:TPU:64, one launch (start us, length us, event | category | flops | bytes accessed | tf_op | source)
XLA Modules:
  0.0 587.6 jit_solution(7296362378037370038)
XLA Ops:
  0.6 0.0 copy-start
  0.6 0.7 compare_and_fusion.1
  1.4 0.3 copy-done
  1.7 0.3 convolution_convert_fusion.1
  2.0 0.0 copy-start.5
  2.0 1.1 all_to_all.40
  3.1 7.8 %all-to-all-start.1 = ((bf16[32,5,1664]{2,1,0:T(8,128)(2,1)}), bf16[32,5,1664]{2,1,0:T(8,128)(2,1)S(1)}, u32[]{:S(2)}, u32[]{:S(2)}) async-start(bf16[32,5,1664]{2,1,0:T(8,128)(2,1)} %all_to_all.40), calls=%async_computation.1 | async-start | bytes 1703936 | tf_op jit(solution)/shard_map/all_to_all | solution.py:102
  11.0 0.3 convolution_convert_fusion.2
  11.3 1.1 all_to_all.38
  12.4 23.9 %all-to-all-done.1 = bf16[32,5,1664]{2,1,0:T(8,128)(2,1)S(1)} async-done(((bf16[32,5,1664]{2,1,0:T(8,128)(2,1)}), bf16[32,5,1664]{2,1,0:T(8,128)(2,1)S(1)}, u32[]{:S(2)}, u32[]{:S(2)}) %all-to-all-start.1) | async-done | bytes 532512 | tf_op jit(solution)/shard_map/all_to_all | solution.py:102
  36.3 4.2 all-to-all-start
  40.5 0.0 copy-start.7
  40.5 0.0 copy-start.8
  40.5 0.0 copy-start.6
  40.5 1.3 convolution_convert_fusion
  41.8 1.2 all_to_all.42
  43.0 1.3 reshape_reshape.7
  44.3 1.3 fusion.37
  46.3 0.3 dynamic-update-slice
  46.6 0.3 dynamic-update-slice.1
  46.9 183.6 %all-reduce.5 = (f32[1664]{0:T(1024)S(1)}, f32[1664]{0:T(1024)S(1)}) all-reduce(f32[1664]{0:T(1024)S(1)} %dynamic-update-slice, f32[1664]{0:T(1024)S(1)} %dynamic-update-slice.1), channel_id=1, replica_groups=mesh['dp'=32,'fsdp'=32] {'fsdp'}, use_global_device_ids=true, to_apply=%add | all-reduce | flops 3328 | bytes 26624
  230.5 0.1 compare_and_fusion
  230.6 0.3 multiply_reduce_fusion
  230.9 10.7 %all-to-all-start.2 = ((bf16[32,5,1664]{2,1,0:T(8,128)(2,1)}), bf16[32,5,1664]{2,1,0:T(8,128)(2,1)S(1)}, u32[]{:S(2)}, u32[]{:S(2)}) async-start(bf16[32,5,1664]{2,1,0:T(8,128)(2,1)} %all_to_all.42), calls=%async_computation.2 | async-start | bytes 1703936 | tf_op jit(solution)/shard_map/all_to_all | solution.py:103
  241.6 0.3 multiply_reduce_fusion.1
  241.9 0.1 rsqrt.27
  242.0 0.1 rsqrt.25
  242.1 1.7 reshape.298
  243.8 1.7 reshape.299
  245.5 4.5 fusion.38
  250.0 2.2 fusion.7
  252.2 1.1 copy.39
  253.3 2.4 all_to_all.48
  255.6 4.0 all-to-all-done.2
  259.7 6.4 %all-to-all-start.5 = ((bf16[32,5,1664]{2,1,0:T(8,128)(2,1)}), bf16[32,5,1664]{2,1,0:T(8,128)(2,1)}, u32[]{:S(2)}, u32[]{:S(2)}) async-start(bf16[32,5,1664]{2,1,0:T(8,128)(2,1)} %all_to_all.48), calls=%async_computation.5 | async-start | bytes 1703936 | tf_op jit(solution)/shard_map/all_to_all | solution.py:117
  266.1 1.5 reshape.292
  267.5 3.2 fusion.14
  270.7 6.3 %multiply_reduce_fusion.3 = (f32[13,128]{1,0:T(8,128)S(1)}, f32[160]{0:T(256)S(1)}, f32[160,13,128]{2,0,1:T(8,128)}) fusion(f32[160,13,128]{2,1,0:T(8,128)S(1)} %copy-done.2, f32[160]{0:T(256)S(1)} %rsqrt.25, f32[13,128]{1,0:T(8,128)S(1)} %bitcast.84, f32[13,160,160]{2,1,0:T(8,128)} %fusion.14, f32[13,160,160]{1,2,0:T(8,128)} %get-tuple-element.25, ...), kind=kOutput, calls=%fused_computation.29 | convolution fusion | flops 89922976 | bytes 5887488 | tf_op jit(solution)/shard_map/hqk,hkd->hqd/dot_general | solution.py:66
  277.0 0.1 div.29
  277.1 1.9 copy.36
  278.9 1.4 reshape.293
  280.3 2.8 multiply_convert_fusion.1
  283.2 10.1 %all-to-all-start.3 = ((bf16[32,5,1664]{2,1,0:T(8,128)(2,1)}), bf16[32,5,1664]{2,1,0:T(8,128)(2,1)}, u32[]{:S(2)}, u32[]{:S(2)}) async-start(bf16[32,5,1664]{2,1,0:T(8,128)(2,1)} %multiply_convert_fusion.1), calls=%async_computation.3 | async-start | bytes 1703936 | tf_op jit(solution)/shard_map/all_to_all | solution.py:115
  293.3 6.2 %multiply_reduce_fusion.2 = (f32[13,128]{1,0:T(8,128)S(1)}, f32[160]{0:T(256)S(1)}, f32[160,13,128]{2,0,1:T(8,128)}) fusion(f32[160,13,128]{2,1,0:T(8,128)} %reshape.299, f32[160]{0:T(256)S(1)} %rsqrt.27, f32[13,128]{1,0:T(8,128)S(1)} %bitcast.82, f32[13,160,160]{2,1,0:T(8,128)} %fusion.14, f32[13,160,160]{1,2,0:T(8,128)} %get-tuple-element.25, ...), kind=kOutput, calls=%fused_computation.28 | convolution fusion | flops 89922976 | bytes 5887488 | tf_op jit(solution)/shard_map/hqk,hqd->hkd/dot_general | solution.py:69
  299.5 0.1 div.31
  299.6 2.9 copy.37
  302.5 1.4 reshape.295
  304.0 1.4 multiply_convert_fusion
  305.3 4.8 all-to-all-done.3
  310.1 5.4 all-to-all-start.4
  316.2 2.2 fusion.6
  318.4 0.2 copy.33
  318.7 1.2 reshape_reshape.6
  319.8 177.4 %all-reduce.4 = (f32[1664]{0:T(1024)S(1)}, f32[1664]{0:T(1024)S(1)}) all-reduce(f32[1664]{0:T(1024)S(1)} %bitcast.86, f32[1664]{0:T(1024)S(1)} %bitcast.87), channel_id=2, replica_groups=mesh['dp'=32,'fsdp'=32] {'fsdp'}, use_global_device_ids=true, to_apply=%region_8.10.clone | all-reduce | flops 3328 | bytes 26624
  497.2 0.1 dynamic-slice.3
  497.3 0.1 dynamic-slice.5
  497.4 83.1 %all-reduce.6 = (f32[52]{0:T(128)}, f32[52]{0:T(128)}) all-reduce(f32[52]{0:T(128)S(1)} %dynamic-slice.3, f32[52]{0:T(128)S(1)} %dynamic-slice.5), channel_id=1, replica_groups=mesh['dp'=32,'fsdp'=32] {'dp'}, use_global_device_ids=true, to_apply=%region_9.11 | all-reduce | flops 104 | bytes 832 | tf_op jit(solution)/shard_map/psum | solution.py:126
  580.5 1.4 all_to_all.50
  581.8 0.9 gather_fusion.2
  582.8 1.4 all_to_all.45
  584.2 0.9 gather_fusion
  585.1 0.2 all_to_all.47
  585.4 0.9 gather_fusion.1
  586.3 1.3 select_bitcast_fusion
  (25 shorter events, 0.1 us)
Async XLA Ops:
  0.6 1.0 copy-start
  2.0 9.0 %copy-start.5 = (bf16[1,1,128,1664]{3,2,1,0:T(8,128)(2,1)S(1)}, bf16[1,1,128,1664]{3,2,1,0:T(8,128)(2,1)}, u32[]{:S(2)}) copy-start(bf16[1,1,128,1664]{3,2,1,0:T(8,128)(2,1)} %param.11) | copy-start | bytes 1277956
  3.1 33.2 %all-to-all-start.1 = ((bf16[32,5,1664]{2,1,0:T(8,128)(2,1)}), bf16[32,5,1664]{2,1,0:T(8,128)(2,1)S(1)}, u32[]{:S(2)}, u32[]{:S(2)}) async-start(bf16[32,5,1664]{2,1,0:T(8,128)(2,1)} %all_to_all.40), calls=%async_computation.1 | async-start | bytes 1703936 | tf_op jit(solution)/shard_map/all_to_all | solution.py:102
  12.4 30.6 %copy-start.4 = (bf16[1,1,160,1664]{3,2,1,0:T(8,128)(2,1)S(1)}, bf16[1,1,160,1664]{3,2,1,0:T(8,128)(2,1)}, u32[]{:S(2)}) copy-start(bf16[1,1,160,1664]{3,2,1,0:T(8,128)(2,1)} %param.19) | copy-start | bytes 1597444
  36.3 194.6 %all-to-all-start = ((bf16[32,5,1664]{2,1,0:T(8,128)(2,1)}), bf16[32,5,1664]{2,1,0:T(8,128)(2,1)S(1)}, u32[]{:S(2)}, u32[]{:S(2)}) async-start(bf16[32,5,1664]{2,1,0:T(8,128)(2,1)} %all_to_all.38), calls=%async_computation | async-start | bytes 1703936 | tf_op jit(solution)/shard_map/all_to_all | solution.py:101
  40.5 5.8 copy-start.7
  40.5 6.1 %copy-start.8 = (f32[52]{0:T(128)S(1)}, f32[52]{0:T(128)}, u32[]{:S(2)}) copy-start(f32[52]{0:T(128)} %param.15) | copy-start | bytes 628
  40.5 190.0 %copy-start.6 = (s32[1,1,160]{2,1,0:T(1,128)S(1)}, s32[1,1,160]{2,1,0:T(1,128)}, u32[]{:S(2)}) copy-start(s32[1,1,160]{2,1,0:T(1,128)} %param.18) | copy-start | bytes 1924
  230.9 28.7 %all-to-all-start.2 = ((bf16[32,5,1664]{2,1,0:T(8,128)(2,1)}), bf16[32,5,1664]{2,1,0:T(8,128)(2,1)S(1)}, u32[]{:S(2)}, u32[]{:S(2)}) async-start(bf16[32,5,1664]{2,1,0:T(8,128)(2,1)} %all_to_all.42), calls=%async_computation.2 | async-start | bytes 1703936 | tf_op jit(solution)/shard_map/all_to_all | solution.py:103
  259.7 23.5 %all-to-all-start.5 = ((bf16[32,5,1664]{2,1,0:T(8,128)(2,1)}), bf16[32,5,1664]{2,1,0:T(8,128)(2,1)}, u32[]{:S(2)}, u32[]{:S(2)}) async-start(bf16[32,5,1664]{2,1,0:T(8,128)(2,1)} %all_to_all.48), calls=%async_computation.5 | async-start | bytes 1703936 | tf_op jit(solution)/shard_map/all_to_all | solution.py:117
  267.5 3.2 copy-start.2
  283.2 10.2 %copy-start.3 = (f32[160,13,128]{2,1,0:T(8,128)S(1)}, f32[160,13,128]{2,1,0:T(8,128)}, u32[]{:S(2)}) copy-start(f32[160,13,128]{2,1,0:T(8,128)} %reshape.298) | copy-start | bytes 3194884
  283.2 27.0 %all-to-all-start.3 = ((bf16[32,5,1664]{2,1,0:T(8,128)(2,1)}), bf16[32,5,1664]{2,1,0:T(8,128)(2,1)}, u32[]{:S(2)}, u32[]{:S(2)}) async-start(bf16[32,5,1664]{2,1,0:T(8,128)(2,1)} %multiply_convert_fusion.1), calls=%async_computation.3 | async-start | bytes 1703936 | tf_op jit(solution)/shard_map/all_to_all | solution.py:115
  305.3 10.9 %copy-start.1 = (bf16[160,13,128]{2,1,0:T(8,128)(2,1)S(1)}, bf16[160,13,128]{2,1,0:T(8,128)(2,1)}, u32[]{:S(2)}) copy-start(bf16[160,13,128]{2,1,0:T(8,128)(2,1)} %reshape.292) | copy-start | bytes 1597444
  310.1 275.0 %all-to-all-start.4 = ((bf16[32,5,1664]{2,1,0:T(8,128)(2,1)}), bf16[32,5,1664]{2,1,0:T(8,128)(2,1)S(1)}, u32[]{:S(2)}, u32[]{:S(2)}) async-start(bf16[32,5,1664]{2,1,0:T(8,128)(2,1)} %multiply_convert_fusion), calls=%async_computation.4 | async-start | bytes 1703936 | tf_op jit(solution)/shard_map/all_to_all | solution.py:116
where the time goes:
time: 589 us; the launch traced here: 588 us
  blocking collectives  444 us (75%)
  starting transfers between devices  44.6 us (8%)
  waiting for transfers between devices  32.8 us (6%)
  local copies, waits for them, and re-layouts  30.6 us (5%)
  matrix products  26.4 us (4%)
  other arithmetic  6.92 us (1%)
    unnamed x2, blocking collectives  361 us
    psum x1, blocking collectives, shards(): totals = lax.psum((shares[0], shares[1]), 'dp')  83.1 us
    all_to_all x1, waiting for transfers between devices, shards(): lax.all_to_all(placed(key_home), 'dp', split_axis=0, concat_axis=0, tiled...  23.9 us
  transfers between devices with their start and end apart: 6, of which 3 were waited for; matrix products, arithmetic and copies ran while one was open for 9% of the time, Pallas kernels for 0%

commit v1 on v0

v1 whole, which is shorter than its diff:
```python
import functools

import jax
import jax.numpy as jnp
from jax import lax
from jax.experimental import pallas as pl
from jax.experimental.pallas import tpu as pltpu
from jax.sharding import PartitionSpec as P

HDIM = 128
TILE = 16
PER = 3
EPS = 1e-06
MASKED = -1e30
F32 = jnp.float32
BF16 = jnp.bfloat16
MESH = pl.DeviceIdType.MESH


def dot(a, b, dims=((1,), (0,))):
    return lax.dot_general(a, b, (dims, ((), ())), preferred_element_type=F32)


def iota(shape, dim):
    return lax.broadcasted_iota(jnp.int32, shape, dim)


def as_column(row):
    n = row.shape[1]
    same = iota((n, n), 0) == iota((n, n), 1)
    return jnp.sum(jnp.where(same, row, 0), axis=1, keepdims=True)


def head_lanes(head):
    start = head * HDIM
    if not isinstance(head, int):
        start = pl.multiple_of(start, HDIM)
    return pl.ds(start, HDIM)


def kernel(
    n_dp, n_fsdp, cap, heads, piece,
    q_hbm, k_hbm, v_hbm, do_hbm, gq_ref, gk_ref, dest_ref, slot_ref, seg_ref,
    att_ref, grad_q_ref, grad_k_ref, grad_v_ref, ggq_ref, ggk_ref,
    q_in, k_in, v_in, do_in,
    pick, unpick, pack_r, unpack_r, bias, inv_q, inv_k,
    fwd_send, fwd_recv, ret_send, ret_recv,
    gtmp, gsend, grecv, gain_q, gain_k,
    part, rs_recv, ar_send, ar_recv,
    dqn, dkn, acc_q, acc_k,
    load_sem, fs_sem, fr_sem, bs_sem, br_sem, gs_sem, gr_sem,
):
    tokens = q_in.shape[0]
    width = q_in.shape[1]
    slots = n_dp * cap
    full = heads // PER
    left = heads % PER
    halves = n_dp // TILE
    hrow = TILE * cap
    scaling = 1.0 / HDIM**0.5
    me_d = lax.axis_index("dp")
    me_f = lax.axis_index("fsdp")

    loads = [
        pltpu.make_async_copy(src, dst, load_sem.at[i])
        for i, (src, dst) in enumerate(
            ((v_hbm, v_in), (q_hbm, q_in), (k_hbm, k_in), (do_hbm, do_in))
        )
    ]
    for load in loads:
        load.start()

    barrier = pltpu.get_barrier_semaphore()

    def greet_dp(s, carry):
        pl.semaphore_signal(
            barrier, inc=1, device_id={"dp": lax.rem(me_d + s, n_dp)}, device_id_type=MESH
        )
        return carry

    def greet_fsdp(s, carry):
        pl.semaphore_signal(
            barrier, inc=1, device_id={"fsdp": lax.rem(me_f + s, n_fsdp)}, device_id_type=MESH
        )
        return carry

    lax.fori_loop(1, n_fsdp, greet_fsdp, 0)
    lax.fori_loop(1, n_dp, greet_dp, 0)

    offset = me_f * piece
    lane0 = lax.rem(offset, HDIM)
    gtmp[...] = jnp.zeros_like(gtmp)
    gtmp[0:1, 0:piece] = gq_ref[...]
    gtmp[1:2, 0:piece] = gk_ref[...]
    placed = pltpu.roll(gtmp[...], lane0, 1)
    gsend[...] = jnp.zeros_like(gsend)
    gsend[0:2, :] = placed[0:2, :HDIM]
    gsend[4:6, :] = placed[0:2, HDIM:]
    grecv[me_f] = gsend[...]

    route = dest_ref[...] * TILE + slot_ref[...]
    rows = iota((n_dp * TILE, tokens), 0)
    route_col = as_column(route)
    cols = iota((tokens, n_dp * TILE), 1)
    for j in range(PER):
        lanes = slice(j * tokens, (j + 1) * tokens)
        pick[:, lanes] = jnp.where(rows == route + j * cap, 1.0, 0.0).astype(BF16)
        unpick[lanes, :] = jnp.where(cols == route_col + j * cap, 1.0, 0.0).astype(BF16)

    def send_tiles(src, dst, first, count, send_sem, recv_sem):
        def one(s, carry):
            peer = lax.rem(me_d + s, n_dp)
            pltpu.make_async_remote_copy(
                src_ref=src.at[peer, pl.ds(first, count)],
                dst_ref=dst.at[me_d, pl.ds(first, count)],
                send_sem=send_sem,
                recv_sem=recv_sem,
                device_id={"dp": peer},
                device_id_type=MESH,
            ).start()
            return carry

        lax.fori_loop(1, n_dp, one, 0)
        dst[me_d, pl.ds(first, count)] = src[me_d, pl.ds(first, count)]

    def wait_tiles(buf, first, count, sem):
        ref = buf.at[pl.ds(0, n_dp - 1), pl.ds(first, count)]
        pltpu.make_async_copy(ref, ref, sem).wait()

    def pack(blocks, tile):
        out = dot(pick[...], jnp.concatenate(blocks, axis=0)).astype(BF16)
        fwd_send[:, tile] = out.reshape(n_dp, TILE, HDIM)

    loads[0].wait()

    def pack_v(t, carry):
        pack([v_in[:, head_lanes(t * PER + j)] for j in range(PER)], t)
        return carry

    lax.fori_loop(0, full, pack_v, 0)

    pl.semaphore_wait(barrier, n_dp + n_fsdp - 2)

    def send_gain(s, carry):
        peer = lax.rem(me_f + s, n_fsdp)
        pltpu.make_async_remote_copy(
            src_ref=gsend,
            dst_ref=grecv.at[me_f],
            send_sem=gs_sem.at[0],
            recv_sem=gr_sem.at[0],
            device_id={"fsdp": peer},
            device_id_type=MESH,
        ).start()
        return carry

    def wait_small(buf, sem, n):
        ref = buf.at[pl.ds(0, n - 1)]
        pltpu.make_async_copy(ref, ref, sem).wait()

    lax.fori_loop(1, n_fsdp, send_gain, 0)
    send_tiles(fwd_send, fwd_recv, 0, full, fs_sem.at[full], fr_sem.at[full])

    big = iota((PER * hrow, TILE * TILE), 0)
    small = iota((PER * hrow, TILE * TILE), 1)
    block, inner_row = big // hrow, big % hrow
    want = (inner_row // cap) * TILE + block * cap + inner_row % cap
    unpack_r[...] = jnp.where(want == small, 1.0, 0.0).astype(BF16)
    small = iota((TILE * TILE, PER * hrow), 0)
    big = iota((TILE * TILE, PER * hrow), 1)
    block, inner_row = big // hrow, big % hrow
    want = (inner_row // cap) * TILE + block * cap + inner_row % cap
    pack_r[...] = jnp.where(want == small, 1.0, 0.0).astype(BF16)
    seg_row = seg_ref[...]
    seg_col = as_column(seg_row)
    bias[...] = jnp.where((seg_col == seg_row) & (seg_col >= 0), 0.0, MASKED)

    def inverse(src, dst):
        total = jnp.zeros((tokens, HDIM), F32)
        for h in range(heads):
            x = src[:, head_lanes(h)].astype(F32)
            total = total + x * x
        mean = jnp.sum(total, axis=1, keepdims=True) * (1.0 / width)
        dst[...] = jnp.broadcast_to(lax.rsqrt(mean + EPS), (tokens, HDIM))

    loads[1].wait()
    inverse(q_in, inv_q)
    loads[2].wait()
    inverse(k_in, inv_k)

    wait_small(grecv, gr_sem.at[0], n_fsdp)
    for h in range(heads):
        for which, dst in ((0, gain_q), (1, gain_k)):
            total = jnp.zeros((1, HDIM), F32)
            for i in range(n_fsdp):
                first = i * piece // HDIM
                last = (i * piece + piece - 1) // HDIM
                if first == h:
                    total = total + grecv[i, which : which + 1, :]
                elif last == h:
                    total = total + grecv[i, which + 4 : which + 5, :]
            dst[h : h + 1, :] = total

    def norm_block(src, inv, gain, h):
        x = src[:, head_lanes(h)].astype(F32)
        return (x * inv[...] * gain[pl.ds(h, 1), :]).astype(BF16)

    def q_block(h):
        return norm_block(q_in, inv_q, gain_q, h)

    def k_block(h):
        return norm_block(k_in, inv_k, gain_k, h)

    def pack_qk(g, carry):
        h = g * PER
        t = full + 2 * g
        pack([q_block(h), k_block(h), q_block(h + 1)], t)
        pack([k_block(h + 1), q_block(h + 2), k_block(h + 2)], t + 1)
        send_tiles(fwd_send, fwd_recv, t, 2, fs_sem.at[g], fr_sem.at[g])
        return carry

    lax.fori_loop(0, full, pack_qk, 0)
    for i in range(left):
        h = full * PER + i
        pack([q_block(h), k_block(h), v_in[:, head_lanes(h)]], 3 * full + i)
    if left:
        send_tiles(
            fwd_send, fwd_recv, 3 * full, left, fs_sem.at[full + 1], fr_sem.at[full + 1]
        )

    def unpack(buf, tile):
        out = []
        for a in range(halves):
            x = buf[a * TILE : (a + 1) * TILE, tile].reshape(TILE * TILE, HDIM)
            out.append(dot(unpack_r[...], x).astype(BF16))
        return [
            jnp.concatenate([o[j * hrow : (j + 1) * hrow] for o in out], axis=0)
            for j in range(PER)
        ]

    def pack_back(blocks, tile):
        for a in range(halves):
            x = jnp.concatenate([b[a * hrow : (a + 1) * hrow] for b in blocks], axis=0)
            out = dot(pack_r[...], x).astype(BF16)
            ret_send[a * TILE : (a + 1) * TILE, tile] = out.reshape(TILE, TILE, HDIM)

    valid = jnp.where(seg_row >= 0, 1.0, 0.0)

    def attend(h, q, k, v):
        do = do_in[:, head_lanes(h)]
        st = dot(k, q, ((1,), (1,))) * scaling + bias[...]
        w = jnp.exp(st - jnp.max(st, axis=0, keepdims=True))
        pt = w * (valid / jnp.sum(w, axis=0, keepdims=True))
        ptb = pt.astype(BF16)
        att_ref[:, head_lanes(h)] = dot(ptb, v, ((0,), (0,))).astype(BF16)
        dpt = dot(v, do, ((1,), (1,)))
        inner = jnp.sum(dpt * pt, axis=0, keepdims=True)
        dst = (pt * (dpt - inner) * scaling).astype(BF16)
        dv = dot(ptb, do).astype(BF16)
        dk = dot(dst, q)
        dq = dot(dst, k, ((0,), (0,)))
        sum_q = jnp.sum(dq * q.astype(F32), axis=0, keepdims=True)
        sum_k = jnp.sum(dk * k.astype(F32), axis=0, keepdims=True)
        part[h + 1, 0:1, :] = sum_q
        part[h + 1, 1:2, :] = sum_k
        part[h, 4:5, :] = sum_q
        part[h, 5:6, :] = sum_k
        return dq.astype(BF16), dk.astype(BF16), dv

    part[...] = jnp.zeros_like(part)
    loads[3].wait()
    wait_tiles(fwd_recv, 0, full, fr_sem.at[full])

    def group(g, carry):
        h = g * PER
        t = full + 2 * g
        wait_tiles(fwd_recv, t, 2, fr_sem.at[g])
        v0, v1, v2 = unpack(fwd_recv, g)
        q0, k0, q1 = unpack(fwd_recv, t)
        k1, q2, k2 = unpack(fwd_recv, t + 1)
        dq0, dk0, dv0 = attend(h, q0, k0, v0)
        dq1, dk1, dv1 = attend(h + 1, q1, k1, v1)
        dq2, dk2, dv2 = attend(h + 2, q2, k2, v2)
        pack_back([dq0, dk0, dq1], 3 * g)
        pack_back([dk1, dq2, dk2], 3 * g + 1)
        pack_back([dv0, dv1, dv2], 3 * g + 2)
        send_tiles(ret_send, ret_recv, 3 * g, 3, bs_sem.at[g], br_sem.at[g])
        return carry

    lax.fori_loop(0, full, group, 0)
    if left:
        wait_tiles(fwd_recv, 3 * full, left, fr_sem.at[full + 1])
        for i in range(left):
            h = full * PER + i
            q, k, v = unpack(fwd_recv, 3 * full + i)
            pack_back(attend(h, q, k, v), 3 * full + i)
        send_tiles(ret_send, ret_recv, 3 * full, left, bs_sem.at[full], br_sem.at[full])

    def scatter(s, carry):
        peer = lax.rem(me_f + s, n_fsdp)
        pltpu.make_async_remote_copy(
            src_ref=part.at[(peer * piece) // HDIM + 1],
            dst_ref=rs_recv.at[me_f],
            send_sem=gs_sem.at[1],
            recv_sem=gr_sem.at[1],
            device_id={"fsdp": peer},
            device_id_type=MESH,
        ).start()
        return carry

    lax.fori_loop(1, n_fsdp, scatter, 0)
    rs_recv[me_f] = part[offset // HDIM + 1]

    def unpack_home(tile):
        x = ret_recv[:, tile].reshape(n_dp * TILE, HDIM)
        out = dot(unpick[...], x)
        return [out[j * tokens : (j + 1) * tokens] for j in range(PER)]

    def keep(h, grad, raw, inv, gain, dst, acc):
        unit = raw[:, head_lanes(h)].astype(F32) * inv[...]
        acc[...] += grad * gain[pl.ds(h, 1), :] * unit
        dst[:, head_lanes(h)] = grad.astype(BF16)

    def keep_q(h, grad):
        keep(h, grad, q_in, inv_q, gain_q, dqn, acc_q)

    def keep_k(h, grad):
        keep(h, grad, k_in, inv_k, gain_k, dkn, acc_k)

    acc_q[...] = jnp.zeros_like(acc_q)
    acc_k[...] = jnp.zeros_like(acc_k)

    def home(g):
        h = g * PER
        wait_tiles(ret_recv, 3 * g, 3, br_sem.at[g])
        dq0, dk0, dq1 = unpack_home(3 * g)
        keep_q(h, dq0)
        keep_k(h, dk0)
        keep_q(h + 1, dq1)
        dk1, dq2, dk2 = unpack_home(3 * g + 1)
        keep_k(h + 1, dk1)
        keep_q(h + 2, dq2)
        keep_k(h + 2, dk2)
        for j, dv in enumerate(unpack_home(3 * g + 2)):
            grad_v_ref[:, head_lanes(h + j)] = dv.astype(BF16)

    def home_step(g, carry):
        home(g)
        return carry

    early = full - 1
    lax.fori_loop(0, early, home_step, 0)

    wait_small(rs_recv, gr_sem.at[1], n_fsdp)
    ar_send[...] = jnp.sum(rs_recv[...], axis=0)

    def share(s, carry):
        pltpu.make_async_remote_copy(
            src_ref=ar_send,
            dst_ref=ar_recv.at[me_d],
            send_sem=gs_sem.at[2],
            recv_sem=gr_sem.at[2],
            device_id={"dp": lax.rem(me_d + s, n_dp)},
            device_id_type=MESH,
        ).start()
        return carry

    lax.fori_loop(1, n_dp, share, 0)
    ar_recv[me_d] = ar_send[...]

    lax.fori_loop(early, full, home_step, 0)

    wait_small(ar_recv, gr_sem.at[2], n_dp)
    total = jnp.sum(ar_recv[...], axis=0)
    gtmp[:, :HDIM] = total
    gtmp[0:2, HDIM:] = total[4:6, :]
    mine = pltpu.roll(gtmp[...], lax.rem(2 * HDIM - lane0, 2 * HDIM), 1)
    ggq_ref[...] = mine[0:1, 0:piece] / gq_ref[...]
    ggk_ref[...] = mine[1:2, 0:piece] / gk_ref[...]

    if left:
        wait_tiles(ret_recv, 3 * full, left, br_sem.at[full])
        for i in range(left):
            h = full * PER + i
            dq, dk, dv = unpack_home(3 * full + i)
            keep_q(h, dq)
            keep_k(h, dk)
            grad_v_ref[:, head_lanes(h)] = dv.astype(BF16)

    for raw, inv, gain, src, acc, dst in (
        (q_in, inv_q, gain_q, dqn, acc_q, grad_q_ref),
        (k_in, inv_k, gain_k, dkn, acc_k, grad_k_ref),
    ):
        mean = jnp.sum(acc[...], axis=1, keepdims=True) * (1.0 / width)
        factor = inv[...]
        for h in range(heads):
            lanes = head_lanes(h)
            unit = raw[:, lanes].astype(F32) * factor
            grad = src[:, lanes].astype(F32) * gain[h : h + 1, :]
            dst[:, lanes] = (factor * (grad - unit * mean)).astype(BF16)

    for g in range(full):
        wait_tiles(fwd_send, full + 2 * g, 2, fs_sem.at[g])
        wait_tiles(ret_send, 3 * g, 3, bs_sem.at[g])
    wait_tiles(fwd_send, 0, full, fs_sem.at[full])
    if left:
        wait_tiles(fwd_send, 3 * full, left, fs_sem.at[full + 1])
        wait_tiles(ret_send, 3 * full, left, bs_sem.at[full])
    wait_small(grecv, gs_sem.at[0], n_fsdp)
    wait_small(rs_recv, gs_sem.at[1], n_fsdp)
    wait_small(ar_recv, gs_sem.at[2], n_dp)


def shards(q_raw, k_raw, v_raw, gain_q, gain_k, dest, slot, recv_image, d_attended):
    tokens, width = q_raw.shape[2:]
    n_dp, n_fsdp = lax.axis_size("dp"), lax.axis_size("fsdp")
    slots = recv_image.shape[2]
    cap = slots // n_dp
    heads = width // HDIM
    piece = gain_q.shape[0]
    full, left = heads // PER, heads % PER
    tiles = 3 * full + left
    vmem = pl.BlockSpec(memory_space=pltpu.VMEM)
    hbm = pl.BlockSpec(memory_space=pl.ANY)
    rows = pltpu.VMEM((tokens, width), BF16)
    moved = pltpu.VMEM((n_dp, tiles, TILE, HDIM), BF16)
    square = pltpu.VMEM((tokens, HDIM), F32)
    sem = pltpu.SemaphoreType.DMA
    hrow = TILE * cap
    grid_rows = (heads + 15) // 8 * 8
    outs = pl.pallas_call(
        functools.partial(kernel, n_dp, n_fsdp, cap, heads, piece),
        out_shape=(
            jax.ShapeDtypeStruct((slots, width), BF16),
            jax.ShapeDtypeStruct((tokens, width), BF16),
            jax.ShapeDtypeStruct((tokens, width), BF16),
            jax.ShapeDtypeStruct((tokens, width), BF16),
            jax.ShapeDtypeStruct((1, piece), F32),
            jax.ShapeDtypeStruct((1, piece), F32),
        ),
        in_specs=[hbm] * 4 + [vmem] * 5,
        out_specs=[vmem] * 6,
        scratch_shapes=[
            rows, rows, rows, pltpu.VMEM((slots, width), BF16),
            pltpu.VMEM((n_dp * TILE, PER * tokens), BF16),
            pltpu.VMEM((PER * tokens, n_dp * TILE), BF16),
            pltpu.VMEM((TILE * TILE, PER * hrow), BF16),
            pltpu.VMEM((PER * hrow, TILE * TILE), BF16),
            pltpu.VMEM((slots, slots), F32),
            square, square,
            moved, moved, moved, moved,
            pltpu.VMEM((8, 2 * HDIM), F32),
            pltpu.VMEM((8, HDIM), F32),
            pltpu.VMEM((n_fsdp, 8, HDIM), F32),
            pltpu.VMEM((grid_rows, HDIM), F32),
            pltpu.VMEM((grid_rows, HDIM), F32),
            pltpu.VMEM((heads + 1, 8, HDIM), F32),
            pltpu.VMEM((n_fsdp, 8, HDIM), F32),
            pltpu.VMEM((8, HDIM), F32),
            pltpu.VMEM((n_dp, 8, HDIM), F32),
            rows, rows, square, square,
            sem((4,)), sem((full + 2,)), sem((full + 2,)), sem((full + 1,)), sem((full + 1,)),
            sem((3,)), sem((3,)),
        ],
        compiler_params=pltpu.CompilerParams(
            collective_id=0, has_side_effects=True, vmem_limit_bytes=48 * 1024 * 1024
        ),
        name="route_attend",
    )(
        q_raw.reshape(tokens, width),
        k_raw.reshape(tokens, width),
        v_raw.reshape(tokens, width),
        d_attended.reshape(slots, width),
        gain_q.reshape(1, piece),
        gain_k.reshape(1, piece),
        dest.reshape(1, tokens),
        slot.reshape(1, tokens),
        recv_image.reshape(1, slots),
    )
    attended, grad_q, grad_k, grad_v, grad_gain_q, grad_gain_k = outs
    return (
        attended.reshape(1, 1, slots, width),
        grad_q.reshape(1, 1, tokens, width),
        grad_k.reshape(1, 1, tokens, width),
        grad_v.reshape(1, 1, tokens, width),
        grad_gain_q.reshape(piece),
        grad_gain_k.reshape(piece),
    )


def solution(mesh):
    token = P("dp", "fsdp", None, None)
    index = P("dp", "fsdp", None)
    return jax.shard_map(
        shards,
        mesh=mesh,
        in_specs=(token, token, token, P("fsdp"), P("fsdp"), index, index, index, token),
        out_specs=(token, token, token, token, P("fsdp"), P("fsdp")),
        check_vma=False,
    )
```

time: 589 us -> 158 us (0.27)
  the two profiles are of different devices: /device:TPU:64 before, /device:TPU:1 now
where the time goes in v1:
time: 158 us; the launch traced here: 157 us
  Pallas kernels  147 us (93%)
  local copies, waits for them, and re-layouts  8.84 us (6%)
    pallas_call x1, Pallas kernels, shards(): pl.pallas_call(functools.partial(kernel, n_dp, n_fsdp, cap, heads, piece)...  147 us
    unnamed x24, local copies, waits for them, and re-layouts  8.84 us

profile of v1, /device:TPU:1, one launch (start us, length us, event | category | flops | bytes accessed | tf_op | source)
XLA Modules:
  0.0 156.9 jit_solution(304709798660971857)
XLA Ops:
  0.6 0.0 copy-start.6
  0.6 0.0 copy-start.7
  0.7 0.0 copy-start.8
  0.7 0.0 copy-start.4
  0.7 0.0 copy-start.5
  0.7 0.6 copy-done.6
  1.3 0.0 copy-done.7
  1.3 0.0 copy-done.8
  1.3 0.0 copy-done.4
  1.4 0.0 copy-done.5
  1.4 0.0 copy-start
  1.4 1.0 copy-done
  2.4 0.0 copy-start.1
  2.4 1.0 copy-done.1
  3.4 0.0 copy-start.2
  3.4 1.0 copy-done.2
  4.4 0.0 copy-start.3
  4.4 1.0 copy-done.3
  5.4 147.4 %route_attend.1 = (bf16[160,1664]{1,0:T(8,128)(2,1)S(1)}, bf16[128,1664]{1,0:T(8,128)(2,1)S(1)}, bf16[128,1664]{1,0:T(8,128)(2,1)S(1)}, bf16[128,1664]{1,0:T(8,1...) custom-call(bf16[128,1664]{1,0:T(8,128)(2,1)S(1)} %bitcast.20, bf16[128,1664]{1,0:T(8,128)(2,1)S(1)} %bitcast.21, ...), custom_call_target="tpu_custom_call" | custom-call | tf_op jit(solution)/shard_map/route_attend/pallas_call | solution.py:430
  152.8 0.8 copy.21
  153.6 0.8 copy.22
  154.4 0.8 copy.23
  155.1 0.8 copy.24
  155.9 0.5 copy.25
  156.4 0.5 copy.26
Async XLA Ops:
  0.6 0.7 copy-start.6
  0.6 0.7 copy-start.7
  0.7 0.7 copy-start.8
  0.7 0.7 copy-start.4
  0.7 0.7 copy-start.5
  1.4 1.0 copy-start
  2.4 1.0 copy-start.1
  3.4 1.0 copy-start.2
  4.4 1.0 copy-start.3

commit v2 on v1

--- a/solution.py
+++ b/solution.py
@@ -41,14 +41,15 @@
 def kernel(
     n_dp, n_fsdp, cap, heads, piece,
     q_hbm, k_hbm, v_hbm, do_hbm, gq_ref, gk_ref, dest_ref, slot_ref, seg_ref,
-    att_ref, grad_q_ref, grad_k_ref, grad_v_ref, ggq_ref, ggk_ref,
+    att_out, grad_q_out, grad_k_out, grad_v_out, ggq_ref, ggk_ref,
     q_in, k_in, v_in, do_in,
-    pick, unpick, pack_r, unpack_r, bias, inv_q, inv_k,
+    att_ref, grad_q_ref, grad_k_ref, grad_v_ref,
+    pick, pick_last, unpick, pack_r, unpack_r, last_r, bias, inv_q, inv_k, inv_rq, inv_rk,
     fwd_send, fwd_recv, ret_send, ret_recv,
     gtmp, gsend, grecv, gain_q, gain_k,
     part, rs_recv, ar_send, ar_recv,
     dqn, dkn, acc_q, acc_k,
-    load_sem, fs_sem, fr_sem, bs_sem, br_sem, gs_sem, gr_sem,
+    load_sem, store_sem, fs_sem, fr_sem, bs_sem, br_sem, gs_sem, gr_sem,
 ):
     tokens = q_in.shape[0]
     width = q_in.shape[1]
@@ -64,7 +65,7 @@
     loads = [
         pltpu.make_async_copy(src, dst, load_sem.at[i])
         for i, (src, dst) in enumerate(
-            ((v_hbm, v_in), (q_hbm, q_in), (k_hbm, k_in), (do_hbm, do_in))
+            ((q_hbm, q_in), (k_hbm, k_in), (v_hbm, v_in), (do_hbm, do_in))
         )
     ]
     for load in loads:
@@ -93,9 +94,8 @@
     gtmp[0:1, 0:piece] = gq_ref[...]
     gtmp[1:2, 0:piece] = gk_ref[...]
     placed = pltpu.roll(gtmp[...], lane0, 1)
-    gsend[...] = jnp.zeros_like(gsend)
     gsend[0:2, :] = placed[0:2, :HDIM]
-    gsend[4:6, :] = placed[0:2, HDIM:]
+    gsend[2:4, :] = placed[0:2, HDIM:]
     grecv[me_f] = gsend[...]
 
     route = dest_ref[...] * TILE + slot_ref[...]
@@ -106,6 +106,35 @@
         lanes = slice(j * tokens, (j + 1) * tokens)
         pick[:, lanes] = jnp.where(rows == route + j * cap, 1.0, 0.0).astype(BF16)
         unpick[lanes, :] = jnp.where(cols == route_col + j * cap, 1.0, 0.0).astype(BF16)
+    pick_last[...] = jnp.where(rows == dest_ref[...] * TILE + (TILE - 1), 1.0, 0.0).astype(BF16)
+
+    def inverse(src, dst):
+        total = jnp.zeros((tokens, HDIM), F32)
+        for h in range(heads):
+            x = src[:, head_lanes(h)].astype(F32)
+            total = total + x * x
+        mean = jnp.sum(total, axis=1, keepdims=True) * (1.0 / width)
+        dst[...] = jnp.broadcast_to(lax.rsqrt(mean + EPS), (tokens, HDIM))
+
+    loads[0].wait()
+    inverse(q_in, inv_q)
+    loads[1].wait()
+    inverse(k_in, inv_k)
+
+    def thirds(value):
+        high = value.astype(BF16)
+        rest = value - high.astype(F32)
+        middle = rest.astype(BF16)
+        low = (rest - middle.astype(F32)).astype(BF16)
+        return high, middle, low
+
+    slot_col = as_column(slot_ref[...])
+    lane = iota((tokens, HDIM), 1)
+    extra = jnp.zeros((tokens, HDIM), F32)
+    for t, inv in enumerate((inv_q, inv_k)):
+        for p, third in enumerate(thirds(inv[...])):
+            extra = jnp.where(lane == (2 * p + t) * cap + slot_col, third.astype(F32), extra)
+    extra = extra.astype(BF16)
 
     def send_tiles(src, dst, first, count, send_sem, recv_sem):
         def one(s, carry):
@@ -127,17 +156,29 @@
         ref = buf.at[pl.ds(0, n_dp - 1), pl.ds(first, count)]
         pltpu.make_async_copy(ref, ref, sem).wait()
 
-    def pack(blocks, tile):
-        out = dot(pick[...], jnp.concatenate(blocks, axis=0)).astype(BF16)
-        fwd_send[:, tile] = out.reshape(n_dp, TILE, HDIM)
-
-    loads[0].wait()
-
-    def pack_v(t, carry):
-        pack([v_in[:, head_lanes(t * PER + j)] for j in range(PER)], t)
-        return carry
-
-    lax.fori_loop(0, full, pack_v, 0)
+    def pack(blocks, tile, last=None):
+        out = dot(pick[...], jnp.concatenate(blocks, axis=0))
+        if last is not None:
+            out = out + dot(pick_last[...], last)
+        fwd_send[:, tile] = out.astype(BF16).reshape(n_dp, TILE, HDIM)
+
+    def q_block(h):
+        return q_in[:, head_lanes(h)]
+
+    def k_block(h):
+        return k_in[:, head_lanes(h)]
+
+    def v_block(h):
+        return v_in[:, head_lanes(h)]
+
+    def pack_group(g, last=None):
+        h = g * PER
+        pack([q_block(h), k_block(h), q_block(h + 1)], 3 * g, last)
+        pack([k_block(h + 1), q_block(h + 2), k_block(h + 2)], 3 * g + 1)
+        pack([v_block(h), v_block(h + 1), v_block(h + 2)], 3 * g + 2)
+
+    loads[2].wait()
+    pack_group(0, extra)
 
     pl.semaphore_wait(barrier, n_dp + n_fsdp - 2)
 
@@ -158,7 +199,19 @@
         pltpu.make_async_copy(ref, ref, sem).wait()
 
     lax.fori_loop(1, n_fsdp, send_gain, 0)
-    send_tiles(fwd_send, fwd_recv, 0, full, fs_sem.at[full], fr_sem.at[full])
+    send_tiles(fwd_send, fwd_recv, 0, 3, fs_sem.at[0], fr_sem.at[0])
+
+    def forward(g, carry):
+        pack_group(g)
+        send_tiles(fwd_send, fwd_recv, 3 * g, 3, fs_sem.at[g], fr_sem.at[g])
+        return carry
+
+    lax.fori_loop(1, full, forward, 0)
+    for i in range(left):
+        h = full * PER + i
+        pack([q_block(h), k_block(h), v_block(h)], 3 * full + i)
+    if left:
+        send_tiles(fwd_send, fwd_recv, 3 * full, left, fs_sem.at[full], fr_sem.at[full])
 
     big = iota((PER * hrow, TILE * TILE), 0)
     small = iota((PER * hrow, TILE * TILE), 1)
@@ -170,22 +223,12 @@
     block, inner_row = big // hrow, big % hrow
     want = (inner_row // cap) * TILE + block * cap + inner_row % cap
     pack_r[...] = jnp.where(want == small, 1.0, 0.0).astype(BF16)
+    small = iota((hrow, TILE * TILE), 1)
+    want = (iota((hrow, TILE * TILE), 0) // cap) * TILE + (TILE - 1)
+    last_r[...] = jnp.where(want == small, 1.0, 0.0).astype(BF16)
     seg_row = seg_ref[...]
     seg_col = as_column(seg_row)
     bias[...] = jnp.where((seg_col == seg_row) & (seg_col >= 0), 0.0, MASKED)
-
-    def inverse(src, dst):
-        total = jnp.zeros((tokens, HDIM), F32)
-        for h in range(heads):
-            x = src[:, head_lanes(h)].astype(F32)
-            total = total + x * x
-        mean = jnp.sum(total, axis=1, keepdims=True) * (1.0 / width)
-        dst[...] = jnp.broadcast_to(lax.rsqrt(mean + EPS), (tokens, HDIM))
-
-    loads[1].wait()
-    inverse(q_in, inv_q)
-    loads[2].wait()
-    inverse(k_in, inv_k)
 
     wait_small(grecv, gr_sem.at[0], n_fsdp)
     for h in range(heads):
@@ -197,45 +240,33 @@
                 if first == h:
                     total = total + grecv[i, which : which + 1, :]
                 elif last == h:
-                    total = total + grecv[i, which + 4 : which + 5, :]
+                    total = total + grecv[i, which + 2 : which + 3, :]
             dst[h : h + 1, :] = total
-
-    def norm_block(src, inv, gain, h):
-        x = src[:, head_lanes(h)].astype(F32)
-        return (x * inv[...] * gain[pl.ds(h, 1), :]).astype(BF16)
-
-    def q_block(h):
-        return norm_block(q_in, inv_q, gain_q, h)
-
-    def k_block(h):
-        return norm_block(k_in, inv_k, gain_k, h)
-
-    def pack_qk(g, carry):
-        h = g * PER
-        t = full + 2 * g
-        pack([q_block(h), k_block(h), q_block(h + 1)], t)
-        pack([k_block(h + 1), q_block(h + 2), k_block(h + 2)], t + 1)
-        send_tiles(fwd_send, fwd_recv, t, 2, fs_sem.at[g], fr_sem.at[g])
-        return carry
-
-    lax.fori_loop(0, full, pack_qk, 0)
-    for i in range(left):
-        h = full * PER + i
-        pack([q_block(h), k_block(h), v_in[:, head_lanes(h)]], 3 * full + i)
-    if left:
-        send_tiles(
-            fwd_send, fwd_recv, 3 * full, left, fs_sem.at[full + 1], fr_sem.at[full + 1]
-        )
 
     def unpack(buf, tile):
         out = []
         for a in range(halves):
             x = buf[a * TILE : (a + 1) * TILE, tile].reshape(TILE * TILE, HDIM)
-            out.append(dot(unpack_r[...], x).astype(BF16))
+            out.append(dot(unpack_r[...], x))
         return [
             jnp.concatenate([o[j * hrow : (j + 1) * hrow] for o in out], axis=0)
             for j in range(PER)
         ]
+
+    def read_inverses():
+        out = []
+        for a in range(halves):
+            x = fwd_recv[a * TILE : (a + 1) * TILE, 0].reshape(TILE * TILE, HDIM)
+            out.append(dot(last_r[...], x))
+        both = jnp.concatenate(out, axis=0)
+        lane = iota((slots, HDIM), 1)
+        at = iota((slots, HDIM), 0) % cap
+        for t, dst in enumerate((inv_rq, inv_rk)):
+            total = jnp.zeros((slots, HDIM), F32)
+            for p in range(3):
+                one = jnp.where(lane == (2 * p + t) * cap + at, both, 0.0)
+                total = total + jnp.sum(one, axis=1, keepdims=True)
+            dst[...] = total
 
     def pack_back(blocks, tile):
         for a in range(halves):
@@ -247,6 +278,9 @@
 
     def attend(h, q, k, v):
         do = do_in[:, head_lanes(h)]
+        q = (q * inv_rq[...] * gain_q[pl.ds(h, 1), :]).astype(BF16)
+        k = (k * inv_rk[...] * gain_k[pl.ds(h, 1), :]).astype(BF16)
+        v = v.astype(BF16)
         st = dot(k, q, ((1,), (1,))) * scaling + bias[...]
         w = jnp.exp(st - jnp.max(st, axis=0, keepdims=True))
         pt = w * (valid / jnp.sum(w, axis=0, keepdims=True))
@@ -262,38 +296,61 @@
         sum_k = jnp.sum(dk * k.astype(F32), axis=0, keepdims=True)
         part[h + 1, 0:1, :] = sum_q
         part[h + 1, 1:2, :] = sum_k
-        part[h, 4:5, :] = sum_q
-        part[h, 5:6, :] = sum_k
+        part[h, 2:3, :] = sum_q
+        part[h, 3:4, :] = sum_k
         return dq.astype(BF16), dk.astype(BF16), dv
 
     part[...] = jnp.zeros_like(part)
     loads[3].wait()
-    wait_tiles(fwd_recv, 0, full, fr_sem.at[full])
-
-    def group(g, carry):
+    wait_tiles(fwd_recv, 0, 3, fr_sem.at[0])
+    read_inverses()
+
+    def group(g):
         h = g * PER
-        t = full + 2 * g
-        wait_tiles(fwd_recv, t, 2, fr_sem.at[g])
-        v0, v1, v2 = unpack(fwd_recv, g)
-        q0, k0, q1 = unpack(fwd_recv, t)
-        k1, q2, k2 = unpack(fwd_recv, t + 1)
+        q0, k0, q1 = unpack(fwd_recv, 3 * g)
+        k1, q2, k2 = unpack(fwd_recv, 3 * g + 1)
+        v0, v1, v2 = unpack(fwd_recv, 3 * g + 2)
         dq0, dk0, dv0 = attend(h, q0, k0, v0)
         dq1, dk1, dv1 = attend(h + 1, q1, k1, v1)
         dq2, dk2, dv2 = attend(h + 2, q2, k2, v2)
         pack_back([dq0, dk0, dq1], 3 * g)
         pack_back([dk1, dq2, dk2], 3 * g + 1)
         pack_back([dv0, dv1, dv2], 3 * g + 2)
+
+    def group_step(g, carry):
+        wait_tiles(fwd_recv, 3 * g, 3, fr_sem.at[g])
+        group(g)
+        return carry
+
+    def back(g, carry):
         send_tiles(ret_send, ret_recv, 3 * g, 3, bs_sem.at[g], br_sem.at[g])
         return carry
 
-    lax.fori_loop(0, full, group, 0)
+    final = full - 1
+    group(0)
+    lax.fori_loop(1, final, group_step, 0)
+    wait_tiles(fwd_recv, 3 * final, 3, fr_sem.at[final])
     if left:
-        wait_tiles(fwd_recv, 3 * full, left, fr_sem.at[full + 1])
-        for i in range(left):
-            h = full * PER + i
-            q, k, v = unpack(fwd_recv, 3 * full + i)
-            pack_back(attend(h, q, k, v), 3 * full + i)
-        send_tiles(ret_send, ret_recv, 3 * full, left, bs_sem.at[full], br_sem.at[full])
+        wait_tiles(fwd_recv, 3 * full, left, fr_sem.at[full])
+    lax.fori_loop(0, final, back, 0)
+    group(final)
+    back(final, 0)
+    for i in range(left):
+        q, k, v = unpack(fwd_recv, 3 * full + i)
+        pack_back(attend(full * PER + i, q, k, v), 3 * full + i)
+
+    stores = [
+        pltpu.make_async_copy(src, dst, store_sem.at[i])
+        for i, (src, dst) in enumerate(
+            (
+                (att_ref, att_out),
+                (grad_v_ref, grad_v_out),
+                (grad_q_ref, grad_q_out),
+                (grad_k_ref, grad_k_out),
+            )
+        )
+    ]
+    stores[0].start()
 
     def scatter(s, carry):
         peer = lax.rem(me_f + s, n_fsdp)
@@ -309,6 +366,8 @@
 
     lax.fori_loop(1, n_fsdp, scatter, 0)
     rs_recv[me_f] = part[offset // HDIM + 1]
+    if left:
+        send_tiles(ret_send, ret_recv, 3 * full, left, bs_sem.at[full], br_sem.at[full])
 
     def unpack_home(tile):
         x = ret_recv[:, tile].reshape(n_dp * TILE, HDIM)
@@ -347,9 +406,6 @@
         home(g)
         return carry
 
-    early = full - 1
-    lax.fori_loop(0, early, home_step, 0)
-
     wait_small(rs_recv, gr_sem.at[1], n_fsdp)
     ar_send[...] = jnp.sum(rs_recv[...], axis=0)
 
@@ -367,15 +423,7 @@
     lax.fori_loop(1, n_dp, share, 0)
     ar_recv[me_d] = ar_send[...]
 
-    lax.fori_loop(early, full, home_step, 0)
-
-    wait_small(ar_recv, gr_sem.at[2], n_dp)
-    total = jnp.sum(ar_recv[...], axis=0)
-    gtmp[:, :HDIM] = total
-    gtmp[0:2, HDIM:] = total[4:6, :]
-    mine = pltpu.roll(gtmp[...], lax.rem(2 * HDIM - lane0, 2 * HDIM), 1)
-    ggq_ref[...] = mine[0:1, 0:piece] / gq_ref[...]
-    ggk_ref[...] = mine[1:2, 0:piece] / gk_ref[...]
+    lax.fori_loop(0, full, home_step, 0)
 
     if left:
         wait_tiles(ret_recv, 3 * full, left, br_sem.at[full])
@@ -386,9 +434,10 @@
             keep_k(h, dk)
             grad_v_ref[:, head_lanes(h)] = dv.astype(BF16)
 
-    for raw, inv, gain, src, acc, dst in (
-        (q_in, inv_q, gain_q, dqn, acc_q, grad_q_ref),
-        (k_in, inv_k, gain_k, dkn, acc_k, grad_k_ref),
+    stores[1].start()
+    for raw, inv, gain, src, acc, dst, store in (
+        (q_in, inv_q, gain_q, dqn, acc_q, grad_q_ref, stores[2]),
+        (k_in, inv_k, gain_k, dkn, acc_k, grad_k_ref, stores[3]),
     ):
         mean = jnp.sum(acc[...], axis=1, keepdims=True) * (1.0 / width)
         factor = inv[...]
@@ -397,17 +446,41 @@
             unit = raw[:, lanes].astype(F32) * factor
             grad = src[:, lanes].astype(F32) * gain[h : h + 1, :]
             dst[:, lanes] = (factor * (grad - unit * mean)).astype(BF16)
+        store.start()
+
+    wait_small(ar_recv, gr_sem.at[2], n_dp)
+    total = jnp.sum(ar_recv[...], axis=0)
+    gtmp[0:2, :HDIM] = total[0:2, :]
+    gtmp[0:2, HDIM:] = total[2:4, :]
+    mine = pltpu.roll(gtmp[...], lax.rem(2 * HDIM - lane0, 2 * HDIM), 1)
+    ggq_ref[...] = mine[0:1, 0:piece] / gq_ref[...]
+    ggk_ref[...] = mine[1:2, 0:piece] / gk_ref[...]
 
     for g in range(full):
-        wait_tiles(fwd_send, full + 2 * g, 2, fs_sem.at[g])
+        wait_tiles(fwd_send, 3 * g, 3, fs_sem.at[g])
         wait_tiles(ret_send, 3 * g, 3, bs_sem.at[g])
-    wait_tiles(fwd_send, 0, full, fs_sem.at[full])
     if left:
-        wait_tiles(fwd_send, 3 * full, left, fs_sem.at[full + 1])
+        wait_tiles(fwd_send, 3 * full, left, fs_sem.at[full])
         wait_tiles(ret_send, 3 * full, left, bs_sem.at[full])
+    for store in stores:
+        store.wait()
     wait_small(grecv, gs_sem.at[0], n_fsdp)
     wait_small(rs_recv, gs_sem.at[1], n_fsdp)
     wait_small(ar_recv, gs_sem.at[2], n_dp)
+
+
+def store_kernel(*refs):
+    sources, targets, held = refs[:6], refs[6:12], refs[12:18]
+    load_sem, store_sem = refs[18:]
+    loads = [pltpu.make_async_copy(sources[i], held[i], load_sem.at[i]) for i in range(6)]
+    stores = [pltpu.make_async_copy(held[i], targets[i], store_sem.at[i]) for i in range(6)]
+    for load in loads:
+        load.start()
+    for load, store in zip(loads, stores):
+        load.wait()
+        store.start()
+    for store in stores:
+        store.wait()
 
 
 def shards(q_raw, k_raw, v_raw, gain_q, gain_k, dest, slot, recv_image, d_attended):
@@ -420,7 +493,7 @@
     full, left = heads // PER, heads % PER
     tiles = 3 * full + left
     vmem = pl.BlockSpec(memory_space=pltpu.VMEM)
-    hbm = pl.BlockSpec(memory_space=pl.ANY)
+    hbm = pl.BlockSpec(memory_space=pltpu.HBM)
     rows = pltpu.VMEM((tokens, width), BF16)
     moved = pltpu.VMEM((n_dp, tiles, TILE, HDIM), BF16)
     square = pltpu.VMEM((tokens, HDIM), F32)
@@ -438,31 +511,34 @@
             jax.ShapeDtypeStruct((1, piece), F32),
         ),
         in_specs=[hbm] * 4 + [vmem] * 5,
-        out_specs=[vmem] * 6,
+        out_specs=[hbm] * 4 + [vmem] * 2,
         scratch_shapes=[
             rows, rows, rows, pltpu.VMEM((slots, width), BF16),
+            pltpu.VMEM((slots, width), BF16), rows, rows, rows,
             pltpu.VMEM((n_dp * TILE, PER * tokens), BF16),
+            pltpu.VMEM((n_dp * TILE, tokens), BF16),
             pltpu.VMEM((PER * tokens, n_dp * TILE), BF16),
             pltpu.VMEM((TILE * TILE, PER * hrow), BF16),
             pltpu.VMEM((PER * hrow, TILE * TILE), BF16),
+            pltpu.VMEM((hrow, TILE * TILE), BF16),
             pltpu.VMEM((slots, slots), F32),
-            square, square,
+            square, square, pltpu.VMEM((slots, HDIM), F32), pltpu.VMEM((slots, HDIM), F32),
             moved, moved, moved, moved,
             pltpu.VMEM((8, 2 * HDIM), F32),
-            pltpu.VMEM((8, HDIM), F32),
-            pltpu.VMEM((n_fsdp, 8, HDIM), F32),
+            pltpu.VMEM((4, HDIM), F32),
+            pltpu.VMEM((n_fsdp, 4, HDIM), F32),
             pltpu.VMEM((grid_rows, HDIM), F32),
             pltpu.VMEM((grid_rows, HDIM), F32),
-            pltpu.VMEM((heads + 1, 8, HDIM), F32),
-            pltpu.VMEM((n_fsdp, 8, HDIM), F32),
-            pltpu.VMEM((8, HDIM), F32),
-            pltpu.VMEM((n_dp, 8, HDIM), F32),
+            pltpu.VMEM((heads + 1, 4, HDIM), F32),
+            pltpu.VMEM((n_fsdp, 4, HDIM), F32),
+            pltpu.VMEM((4, HDIM), F32),
+            pltpu.VMEM((n_dp, 4, HDIM), F32),
             rows, rows, square, square,
-            sem((4,)), sem((full + 2,)), sem((full + 2,)), sem((full + 1,)), sem((full + 1,)),
+            sem((4,)), sem((4,)), sem((full + 1,)), sem((full + 1,)), sem((full + 1,)), sem((full + 1,)),
             sem((3,)), sem((3,)),
         ],
         compiler_params=pltpu.CompilerParams(
-            collective_id=0, has_side_effects=True, vmem_limit_bytes=48 * 1024 * 1024
+            collective_id=0, has_side_effects=True, vmem_limit_bytes=56 * 1024 * 1024
         ),
         name="route_attend",
     )(
@@ -476,6 +552,15 @@
         slot.reshape(1, tokens),
         recv_image.reshape(1, slots),
     )
+    outs = pl.pallas_call(
+        store_kernel,
+        out_shape=tuple(jax.ShapeDtypeStruct(o.shape, o.dtype) for o in outs),
+        in_specs=[pl.BlockSpec(memory_space=pl.ANY)] * 6,
+        out_specs=[pl.BlockSpec(memory_space=pl.ANY)] * 6,
+        scratch_shapes=[pltpu.VMEM(o.shape, o.dtype) for o in outs] + [sem((6,)), sem((6,))],
+        compiler_params=pltpu.CompilerParams(vmem_limit_bytes=56 * 1024 * 1024),
+        name="store",
+    )(*outs)
     attended, grad_q, grad_k, grad_v, grad_gain_q, grad_gain_k = outs
     return (
         attended.reshape(1, 1, slots, width),

time: 158 us -> 113 us (0.72)
  Pallas kernels: 147 us -> 112 us
  local copies, waits for them, and re-layouts: 8.84 us -> 0 us
    pallas_call x1, Pallas kernels: 147 us -> 110 us  [shards(): pl.pallas_call(functools.partial(kernel, n_dp, n_fsdp, cap, heads, piece)...]
    unnamed x24 -> x0, local copies, waits for them, and re-layouts: 8.84 us -> none
    pallas_call x0 -> x1, Pallas kernels: none -> 2.37 us  [shards(): pl.pallas_call(store_kernel, out_shape=tuple((jax.ShapeDtypeStruct(o.shap...]
where the time goes in v2:
time: 113 us
  Pallas kernels  112 us (99%)
    pallas_call x1, Pallas kernels, shards(): pl.pallas_call(functools.partial(kernel, n_dp, n_fsdp, cap, heads, piece)...  110 us
    pallas_call x1, Pallas kernels, shards(): pl.pallas_call(store_kernel, out_shape=tuple((jax.ShapeDtypeStruct(o.shap...  2.37 us

profile of v2, /device:TPU:1, one launch (start us, length us, event | category | flops | bytes accessed | tf_op | source)
XLA Modules:
  0.0 112.6 jit_solution(2381853605730055752)
XLA Ops:
  0.6 109.6 %route_attend.1 = (bf16[160,1664]{1,0:T(8,128)(2,1)}, bf16[128,1664]{1,0:T(8,128)(2,1)}, bf16[128,1664]{1,0:T(8,128)(2,1)}, bf16[128,1664]{1,0:T(8,128)(2,1)}, f32[1,52]{1,0:T(1,128)}, /*index=5*/f32[1,52]{1,0:T(1,128)}) custom-call(bf16[128,1664]{1,0:T(8,128)(2,1)} %bitcast.16, bf16[128,1664]{1,0:T(8,128)(2,1)} %bitcast.17, bf16[128,1664]{1,0:T(8,128)(2,1)} %bitcast.18, ...), custom_call_target="tpu_custom_call" | custom-call | tf_op jit(solution)/shard_map/route_attend/pallas_call | solution.py:503
  110.2 2.4 %store.1 = (bf16[160,1664]{1,0:T(8,128)(2,1)}, bf16[128,1664]{1,0:T(8,128)(2,1)}, bf16[128,1664]{1,0:T(8,128)(2,1)}, bf16[128,1664]{1,0:T(8,128)(2,1)}, f32[1,52]{1,0:T(1,128)}, /*index=5*/f32[1,52]{1,0:T(1,128)}) custom-call(bf16[160,1664]{1,0:T(8,128)(2,1)} %get-tuple-element.18.refs_0_, bf16[128,1664]{1,0:T(8,128)(2,1)} %get-tuple-element.19.refs_1_, ...), custom_call_target="tpu_custom_call" | custom-call | tf_op jit(solution)/shard_map/store/pallas_call | solution.py:555

commit v3 on v2

--- a/solution.py
+++ b/solution.py
@@ -40,9 +40,9 @@
 
 def kernel(
     n_dp, n_fsdp, cap, heads, piece,
-    q_hbm, k_hbm, v_hbm, do_hbm, gq_ref, gk_ref, dest_ref, slot_ref, seg_ref,
+    q_hbm, k_hbm, v_hbm, do_hbm, gq_hbm, gk_hbm, dest_hbm, slot_hbm, seg_hbm,
     att_out, grad_q_out, grad_k_out, grad_v_out, ggq_ref, ggk_ref,
-    q_in, k_in, v_in, do_in,
+    q_in, k_in, v_in, do_in, gq_ref, gk_ref, dest_ref, slot_ref, seg_ref,
     att_ref, grad_q_ref, grad_k_ref, grad_v_ref,
     pick, pick_last, unpick, pack_r, unpack_r, last_r, bias, inv_q, inv_k, inv_rq, inv_rk,
     fwd_send, fwd_recv, ret_send, ret_recv,
@@ -65,10 +65,16 @@
     loads = [
         pltpu.make_async_copy(src, dst, load_sem.at[i])
         for i, (src, dst) in enumerate(
-            ((q_hbm, q_in), (k_hbm, k_in), (v_hbm, v_in), (do_hbm, do_in))
+            (
+                (q_hbm, q_in), (k_hbm, k_in), (v_hbm, v_in), (do_hbm, do_in),
+                (gq_hbm, gq_ref), (gk_hbm, gk_ref),
+                (dest_hbm, dest_ref), (slot_hbm, slot_ref), (seg_hbm, seg_ref),
+            )
         )
     ]
-    for load in loads:
+    for load in loads[4:]:
+        load.start()
+    for load in loads[:4]:
         load.start()
 
     barrier = pltpu.get_barrier_semaphore()
@@ -85,8 +91,10 @@
         )
         return carry
 
+    lax.fori_loop(1, n_dp, greet_dp, 0)
     lax.fori_loop(1, n_fsdp, greet_fsdp, 0)
-    lax.fori_loop(1, n_dp, greet_dp, 0)
+    for load in loads[4:]:
+        load.wait()
 
     offset = me_f * piece
     lane0 = lax.rem(offset, HDIM)
@@ -328,11 +336,19 @@
 
     final = full - 1
     group(0)
-    lax.fori_loop(1, final, group_step, 0)
+    group_step(1, 0)
+
+    def later(g, carry):
+        wait_tiles(fwd_recv, 3 * g, 3, fr_sem.at[g])
+        back(g - 2, 0)
+        group(g)
+        return carry
+
+    lax.fori_loop(2, final, later, 0)
     wait_tiles(fwd_recv, 3 * final, 3, fr_sem.at[final])
     if left:
         wait_tiles(fwd_recv, 3 * full, left, fr_sem.at[full])
-    lax.fori_loop(0, final, back, 0)
+    lax.fori_loop(final - 2, final, back, 0)
     group(final)
     back(final, 0)
     for i in range(left):
@@ -510,10 +526,13 @@
             jax.ShapeDtypeStruct((1, piece), F32),
             jax.ShapeDtypeStruct((1, piece), F32),
         ),
-        in_specs=[hbm] * 4 + [vmem] * 5,
+        in_specs=[hbm] * 9,
         out_specs=[hbm] * 4 + [vmem] * 2,
         scratch_shapes=[
             rows, rows, rows, pltpu.VMEM((slots, width), BF16),
+            pltpu.VMEM((1, piece), F32), pltpu.VMEM((1, piece), F32),
+            pltpu.VMEM((1, tokens), jnp.int32), pltpu.VMEM((1, tokens), jnp.int32),
+            pltpu.VMEM((1, slots), jnp.int32),
             pltpu.VMEM((slots, width), BF16), rows, rows, rows,
             pltpu.VMEM((n_dp * TILE, PER * tokens), BF16),
             pltpu.VMEM((n_dp * TILE, tokens), BF16),
@@ -534,7 +553,7 @@
             pltpu.VMEM((4, HDIM), F32),
             pltpu.VMEM((n_dp, 4, HDIM), F32),
             rows, rows, square, square,
-            sem((4,)), sem((4,)), sem((full + 1,)), sem((full + 1,)), sem((full + 1,)), sem((full + 1,)),
+            sem((9,)), sem((4,)), sem((full + 1,)), sem((full + 1,)), sem((full + 1,)), sem((full + 1,)),
             sem((3,)), sem((3,)),
         ],
         compiler_params=pltpu.CompilerParams(

time: 113 us -> 126 us (1.12)
  Pallas kernels: 112 us -> 125 us
    pallas_call x1, Pallas kernels: 110 us -> 122 us  [shards(): pl.pallas_call(functools.partial(kernel, n_dp, n_fsdp, cap, heads, piece)...]
where the time goes in v3:
time: 126 us; the launch traced here: 125 us
  Pallas kernels  125 us (99%)
    pallas_call x1, Pallas kernels, shards(): pl.pallas_call(functools.partial(kernel, n_dp, n_fsdp, cap, heads, piece)...  122 us

profile of v3, /device:TPU:1, one launch (start us, length us, event | category | flops | bytes accessed | tf_op | source)
XLA Modules:
  0.0 125.5 jit_solution(4088088765256982032)
XLA Ops:
  0.6 122.5 %route_attend.1 = (bf16[160,1664]{1,0:T(8,128)(2,1)}, bf16[128,1664]{1,0:T(8,128)(2,1)}, bf16[128,1664]{1,0:T(8,128)(2,1)}, bf16[128,1664]{1,0:T(8,128)(2,1)}, f32[1,52]{1,0:T(1,128)}, /*index=5*/f32[1,52]{1,0:T(1,128)}) custom-call(bf16[128,1664]{1,0:T(8,128)(2,1)} %bitcast.16, bf16[128,1664]{1,0:T(8,128)(2,1)} %bitcast.17, bf16[128,1664]{1,0:T(8,128)(2,1)} %bitcast.18, ...), custom_call_target="tpu_custom_call" | custom-call | tf_op jit(solution)/shard_map/route_attend/pallas_call | solution.py:519
  123.1 2.4 %store.1 = (bf16[160,1664]{1,0:T(8,128)(2,1)}, bf16[128,1664]{1,0:T(8,128)(2,1)}, bf16[128,1664]{1,0:T(8,128)(2,1)}, bf16[128,1664]{1,0:T(8,128)(2,1)}, f32[1,52]{1,0:T(1,128)}, /*index=5*/f32[1,52]{1,0:T(1,128)}) custom-call(bf16[160,1664]{1,0:T(8,128)(2,1)} %get-tuple-element.18.refs_0_, bf16[128,1664]{1,0:T(8,128)(2,1)} %get-tuple-element.19.refs_1_, ...), custom_call_target="tpu_custom_call" | custom-call | tf_op jit(solution)/shard_map/store/pallas_call | solution.py:574
